TPU v7x, 32 devices: a whole 2x2x4 slice. The times are simulated.
32 devices in a mesh: ta: 8 (over z, x), sa: 4 (over y, core).
Axes of the slice: x: 2, y: 2, z: 4, core: 2. Of those that a mesh axis runs over, the one named last changes fastest.
Arguments:
- adjoint_in: float32 [3, 2, 48, 8, 64, 128], P(None, None, None, 'sa', 'ta'), may hold values from -6 to 6
- links_late: float32 [4, 3, 3, 2, 8, 64, 128], P(None, None, None, None, 'sa', 'ta'), may hold values from -2.4 to 2.4
- links_mid: float32 [4, 3, 3, 2, 8, 64, 128], P(None, None, None, None, 'sa', 'ta'), may hold values from -2.4 to 2.4
- src_value: float32 [3, 2, 48, 4096], P(None, None, None, ('ta', 'sa')), may hold values from -6 to 6
- src_coord: int32 [4, 4096], P(None, ('ta', 'sa')), may hold values from 0 to 63, as said below
Outputs:
- section_two: float32 [3, 2, 48, 8, 64, 128], P(None, None, None, 'sa', 'ta')
- section_one: float32 [3, 2, 48, 8, 64, 128], P(None, None, None, 'sa', 'ta')
Inputs may be any that keep to these rules, and one draw needn't show every extreme that they name: `src_coord`: the 128 records that lie on the device at position i of ta have time coordinates from i * 8 to (i + 1) * 8 - 1. Among the records of one device at most 64 have x coordinates in the planes of one index of sa (x // 2); for every position of ta, some index of sa receives exactly 64 records from every device at that position. Several records may name the same site.
All inputs are finite; a program needn't handle non-finite values.
Results may differ from a plain program's by a relative error of at most 0.0001.
Values sent between devices are 32-bit elements; how exact they have to be, the bound alone decides.
A program may use at most 128 MiB of HBM per device.

v0:
```python
import functools

import jax
import jax.numpy as jnp
from jax import lax
from jax.experimental import pallas as pl
from jax.experimental.pallas import tpu as pltpu
from jax.sharding import PartitionSpec as P

EXTENT_Z = 8
COLS = 4

flow_step = 0.0625
coef_late = 0.75 * flow_step
coef_mid = 8.0 / 9.0 * flow_step
MESH = pl.DeviceIdType.MESH


def mac(acc, link, vec, dagger):
    for r in range(3):
        for c in range(3):
            m_re = link(c, r, 0) if dagger else link(r, c, 0)
            m_im = link(c, r, 1) if dagger else link(r, c, 1)
            for j in range(COLS):
                v_re, v_im = vec[2 * c][j], vec[2 * c + 1][j]
                a_re = acc[2 * r][j] + m_re * v_re
                a_im = acc[2 * r + 1][j] + m_re * v_im
                if dagger:
                    acc[2 * r][j] = a_re + m_im * v_im
                    acc[2 * r + 1][j] = a_im - m_im * v_re
                else:
                    acc[2 * r][j] = a_re - m_im * v_im
                    acc[2 * r + 1][j] = a_im + m_im * v_re


def kernel(
    n_ta, n_sa,
    adj, late, mid, val, coord,
    two, one,
    top, inj, vals, keys, key_row, val_hi, val_lo,
    xh, ts, th, lts, lth, lxh, back,
    send, recv, lsend, lrecv, vsend, vrecv,
):
    ta, sa = lax.axis_index("ta"), lax.axis_index("sa")
    t_up, t_dn = lax.rem(ta + 1, n_ta), lax.rem(ta + n_ta - 1, n_ta)
    x_up, x_dn = lax.rem(sa + 1, n_sa), lax.rem(sa + n_sa - 1, n_sa)
    chunks = adj.shape[1] // COLS
    records = val.shape[1]
    planes = 2 * n_sa
    links = (late, mid)

    barrier = pltpu.get_barrier_semaphore()
    for step in range(1, n_sa):
        pl.semaphore_signal(
            barrier, inc=1, device_id={"sa": lax.rem(sa + step, n_sa)}, device_id_type=MESH
        )
    for other in (t_up, t_dn):
        pl.semaphore_signal(barrier, inc=1, device_id={"ta": other}, device_id_type=MESH)
    pl.semaphore_wait(barrier, n_sa + 1)

    def remote(src, dst, s, r, where):
        return pltpu.make_async_remote_copy(
            src_ref=src, dst_ref=dst, send_sem=s, recv_sem=r, device_id=where, device_id_type=MESH
        )

    def x_copy(lap, way, k):
        field = adj if lap == 0 else two
        cut = pl.ds(k * COLS, COLS)
        return remote(
            field.at[:, cut, way], xh.at[lap, way, :, cut],
            send.at[lap, way, k], recv.at[lap, way, k], {"sa": x_up if way else x_dn},
        )

    def t_copy(lap, way, k):
        return remote(
            ts.at[lap, way, k], th.at[lap, way, k],
            send.at[lap, 2 + way, k], recv.at[lap, 2 + way, k], {"ta": t_up if way else t_dn},
        )

    def lx_copy(lap):
        return remote(
            links[lap].at[1, :, 1], lxh.at[lap], lsend.at[lap, 0], lrecv.at[lap, 0], {"sa": x_up}
        )

    def lt_copy(lap):
        return remote(lts.at[lap], lth.at[lap], lsend.at[lap, 1], lrecv.at[lap, 1], {"ta": t_up})

    core = lax.rem(sa, 2)
    chip = sa // 2
    n_chip = n_sa // 2
    buddy = sa + 1 - 2 * core

    def rec_copies(kind, step):
        if kind == 0:
            peer = lax.rem(chip + step, n_chip) * 2 + core
            src_v, src_k = vals.at[0, 0], keys.at[0, 0]
        else:
            peer = buddy
            src_v, src_k = vals.at[0, step], keys.at[0, step]
        return (
            remote(src_v, vals.at[kind, step], vsend.at[kind, step, 0], vrecv.at[kind, step, 0], {"sa": peer}),
            remote(src_k, keys.at[kind, step], vsend.at[kind, step, 1], vrecv.at[kind, step, 1], {"sa": peer}),
        )

    vals[0, 0] = val[...]
    key = (coord[1:2, :] * 8 + coord[0:1, :] - ta * 8) * 128 + coord[2:3, :] * EXTENT_Z + coord[3:4, :]
    keys[0, 0] = jnp.broadcast_to(key, (8, records))
    for step in range(1, n_chip):
        for c in rec_copies(0, step):
            c.start()
    for c in rec_copies(1, 0):
        c.start()
    lx_copy(0).start()

    @pl.loop(0, chunks)
    def _(k):
        x_copy(0, 0, k).start()
        x_copy(0, 1, k).start()

    for lap in range(2):
        flat = links[lap].reshape(4 * 18 * 2 * 8, 128)
        lts[lap] = flat[pl.ds(7, 40, stride=8), :]
        lt_copy(lap).start()
    lx_copy(1).start()

    for step in range(1, n_chip):
        for c in rec_copies(0, step):
            c.wait_recv()
        for c in rec_copies(1, step):
            c.start()
    for step in range(n_chip):
        for c in rec_copies(1, step):
            c.wait_recv()
    for kind in range(2):
        for step in range(n_chip):
            at = (kind * n_chip + step) * records
            whole = vals[kind, step]
            high = whole.astype(jnp.bfloat16)
            val_hi[:, at : at + records] = high
            val_lo[:, at : at + records] = (whole - high.astype(jnp.float32)).astype(jnp.bfloat16)
            key_row[:, at : at + records] = keys[kind, step]

    top_flat = top.reshape(288 * 16, 128)
    adj_flat = adj.reshape(288 * 16, 128)
    width = key_row.shape[1]
    dims = (((1,), (1,)), ((), ()))

    @pl.loop(0, 4)
    def _(pair):
        for plane in range(4):
            if plane < 2:
                x_at = sa * 2 + plane
            elif plane == 2:
                x_at = x_up * 2
            else:
                x_at = x_dn * 2 + 1
            first = (x_at * 8 + pair * 2) * 128
            site = lax.broadcasted_iota(jnp.int32, (256, width), 0) + first
            hot = jnp.where(site == key_row[0:1, :], 1.0, 0.0).astype(jnp.bfloat16)
            got = lax.dot_general(val_hi[...], hot, dims, preferred_element_type=jnp.float32)
            got = got + lax.dot_general(val_lo[...], hot, dims, preferred_element_type=jnp.float32)
            for half in range(2):
                part = got[:, half * 128 : half * 128 + 128]
                t_at = pair * 2 + half
                if plane < 2:
                    rows = pl.ds(plane * 8 + t_at, 288, stride=16)
                    top_flat[rows, :] = adj_flat[rows, :] + part
                else:
                    inj.at[plane - 2].reshape(288 * 8, 128)[pl.ds(t_at, 288, stride=8), :] = part

    sign_dn = jnp.where(ta == 0, -1.0, 1.0).astype(jnp.float32)
    sign_up = jnp.where(ta == n_ta - 1, -1.0, 1.0).astype(jnp.float32)

    def send_time(lap, k):
        flat = (top if lap == 0 else two).reshape(288 * 16, 128)
        for comp in range(6):
            base = comp * 48 * 16 + k * COLS * 16
            ts[lap, 0, k, comp] = flat[pl.ds(base, 2 * COLS, stride=8), :] * sign_dn
            ts[lap, 1, k, comp] = flat[pl.ds(base + 7, 2 * COLS, stride=8), :] * sign_up
        t_copy(lap, 0, k).start()
        t_copy(lap, 1, k).start()

    @pl.loop(0, chunks)
    def _(k):
        send_time(0, k)

    row = lax.broadcasted_iota(jnp.int32, (8, 128), 0)
    z_at = lax.rem(lax.broadcasted_iota(jnp.int32, (8, 128), 1), EXTENT_Z)

    def y_ahead(a):
        return pltpu.roll(a, 128 - EXTENT_Z, 1)

    def y_behind(a):
        return pltpu.roll(a, EXTENT_Z, 1)

    def z_ahead(a):
        return jnp.where(z_at == EXTENT_Z - 1, pltpu.roll(a, EXTENT_Z - 1, 1), pltpu.roll(a, 127, 1))

    def z_behind(a):
        return jnp.where(z_at == 0, pltpu.roll(a, 129 - EXTENT_Z, 1), pltpu.roll(a, 1, 1))

    for lap in range(2):
        lx_copy(lap).wait_recv()
        lt_copy(lap).wait_recv()

        @pl.loop(0, 18)
        def _(e):
            link = links[lap]
            for x in range(2):
                edge = lth[lap, pl.ds(e * 2 + x, 1), :]
                back[lap, 0, e, x] = jnp.where(row == 0, edge, pltpu.roll(link[0, e, x], 1, 0))
                back[lap, 1, e, x] = lxh[lap, e] if x == 0 else link[1, e, 0]
                back[lap, 2, e, x] = y_behind(link[2, e, x])
                back[lap, 3, e, x] = z_behind(link[3, e, x])

    def laplacian(lap, k, x):
        field = top if lap == 0 else two
        link = links[lap]

        def ahead(mu):
            return lambda r, c, p: link[mu, (r * 3 + c) * 2 + p, x]

        def behind(mu):
            return lambda r, c, p: back[lap, mu, (r * 3 + c) * 2 + p, x]

        def here(plane):
            return [[field[q, k * COLS + j, plane] for j in range(COLS)] for q in range(6)]

        def halo(way):
            vec = [[xh[lap, way, q, k * COLS + j] for j in range(COLS)] for q in range(6)]
            if lap == 0:
                side = 0 if way == 0 else 1
                vec = [
                    [vec[q][j] + inj[side, q * 48 + k * COLS + j] for j in range(COLS)] for q in range(6)
                ]
            return vec

        def moved(f, vec):
            return [[f(a) for a in line] for line in vec]

        def time(way, vec):
            edge = 7 if way == 0 else 0
            turn = 7 if way == 0 else 1
            return [
                [
                    jnp.where(
                        row == edge,
                        th[lap, way, k, q, pl.ds(2 * j + x, 1), :],
                        pltpu.roll(vec[q][j], turn, 0),
                    )
                    for j in range(COLS)
                ]
                for q in range(6)
            ]

        centre = here(x)
        acc = [[-8.0 * a for a in line] for line in centre]
        mac(acc, ahead(2), moved(y_ahead, centre), False)
        mac(acc, behind(2), moved(y_behind, centre), True)
        mac(acc, ahead(3), moved(z_ahead, centre), False)
        mac(acc, behind(3), moved(z_behind, centre), True)
        mac(acc, ahead(0), time(0, centre), False)
        mac(acc, behind(0), time(1, centre), True)
        mac(acc, ahead(1), here(1) if x == 0 else halo(0), False)
        mac(acc, behind(1), halo(1) if x == 0 else here(0), True)
        return acc

    def arrive(lap, k):
        for way in range(2):
            x_copy(lap, way, k).wait_recv()
            t_copy(lap, way, k).wait_recv()

    @pl.loop(0, chunks)
    def _(k):
        arrive(0, k)
        for x in range(2):
            acc = laplacian(0, k, x)
            for q in range(6):
                for j in range(COLS):
                    two[q, k * COLS + j, x] = coef_late * acc[q][j]
        x_copy(1, 0, k).start()
        x_copy(1, 1, k).start()
        send_time(1, k)

    @pl.loop(0, chunks)
    def _(k):
        arrive(1, k)
        for x in range(2):
            acc = laplacian(1, k, x)
            for q in range(6):
                for j in range(COLS):
                    one[q, k * COLS + j, x] = top[q, k * COLS + j, x] + coef_mid * acc[q][j]

    for step in range(n_chip):
        for c in rec_copies(1, step):
            c.wait_send()
        if step:
            for c in rec_copies(0, step):
                c.wait_send()
    for lap in range(2):
        lx_copy(lap).wait_send()
        lt_copy(lap).wait_send()

        @pl.loop(0, chunks)
        def _(k):
            for way in range(2):
                x_copy(lap, way, k).wait_send()
                t_copy(lap, way, k).wait_send()


def shards(n_ta, n_sa, adjoint_in, links_late, links_mid, src_value, src_coord):
    cols = adjoint_in.shape[2]
    chunks = cols // COLS
    records = src_value.shape[3]
    f32 = jnp.float32
    adj = adjoint_in.reshape(6, cols, 2, 8, 128)
    late = links_late.reshape(4, 18, 2, 8, 128)
    mid = links_mid.reshape(4, 18, 2, 8, 128)
    val = src_value.reshape(6 * cols, records)
    width = n_sa * records
    dma = pltpu.SemaphoreType.DMA
    vmem = pl.BlockSpec(memory_space=pltpu.VMEM)
    two, one = pl.pallas_call(
        functools.partial(kernel, n_ta, n_sa),
        out_shape=(jax.ShapeDtypeStruct(adj.shape, f32), jax.ShapeDtypeStruct(adj.shape, f32)),
        in_specs=[vmem] * 5,
        out_specs=(vmem, vmem),
        scratch_shapes=[
            pltpu.VMEM(adj.shape, f32),
            pltpu.VMEM((2, 6 * cols, 8, 128), f32),
            pltpu.VMEM((2, n_sa // 2, 6 * cols, records), f32),
            pltpu.VMEM((2, n_sa // 2, 8, records), jnp.int32),
            pltpu.VMEM((8, width), jnp.int32),
            pltpu.VMEM((6 * cols, width), jnp.bfloat16),
            pltpu.VMEM((6 * cols, width), jnp.bfloat16),
            pltpu.VMEM((2, 2, 6, cols, 8, 128), f32),
            pltpu.VMEM((2, 2, chunks, 6, 2 * COLS, 128), f32),
            pltpu.VMEM((2, 2, chunks, 6, 2 * COLS, 128), f32),
            pltpu.VMEM((2, 40, 128), f32),
            pltpu.VMEM((2, 40, 128), f32),
            pltpu.VMEM((2, 18, 8, 128), f32),
            pltpu.VMEM((2, 4, 18, 2, 8, 128), f32),
            dma((2, 4, chunks)),
            dma((2, 4, chunks)),
            dma((2, 2)),
            dma((2, 2)),
            dma((2, n_sa // 2, 2)),
            dma((2, n_sa // 2, 2)),
        ],
        compiler_params=pltpu.CompilerParams(
            collective_id=0, has_side_effects=True, vmem_limit_bytes=52 * 1024 * 1024
        ),
    )(adj, late, mid, val, src_coord)
    return two.reshape(adjoint_in.shape), one.reshape(adjoint_in.shape)


def solution(mesh):
    return jax.shard_map(
        functools.partial(shards, mesh.shape["ta"], mesh.shape["sa"]),
        mesh=mesh,
        in_specs=(
            P(None, None, None, "sa", "ta", None),
            P(None, None, None, None, "sa", "ta", None),
            P(None, None, None, None, "sa", "ta", None),
            P(None, None, None, ("ta", "sa")),
            P(None, ("ta", "sa")),
        ),
        out_specs=(P(None, None, None, "sa", "ta", None), P(None, None, None, "sa", "ta", None)),
        check_vma=False,
    )
```

profile of v0, /device:TPU:1, one launch (start us, length us, event | category | flops | bytes accessed | tf_op | source)
XLA Modules:
  0.0 78.8 jit_solution(11988465536566110538)
XLA Ops:
  0.6 0.0 copy-start
  0.6 1.1 %copy-done = f32[4,3,3,2,2,8,128]{6,5,4,3,2,1,0:T(8,128)S(1)} copy-done((f32[4,3,3,2,2,8,128]{6,5,4,3,2,1,0:T(8,128)S(1)}, f32[4,3,3,2,2,8,128]{6,5,4,3,2,1,0:T(8,128)}, u32[]{:S(2)}) %copy-start) | copy-done | bytes 589848
  1.7 0.0 copy-start.1
  1.7 1.1 %copy-done.1 = f32[4,3,3,2,2,8,128]{6,5,4,3,2,1,0:T(8,128)S(1)} copy-done((f32[4,3,3,2,2,8,128]{6,5,4,3,2,1,0:T(8,128)S(1)}, f32[4,3,3,2,2,8,128]{6,5,4,3,2,1,0:T(8,128)}, u32[]{:S(2)}) %copy-start.1) | copy-done | bytes 589848
  2.8 0.0 copy-start.2
  2.8 0.9 %copy-done.2 = f32[3,2,48,128]{3,2,1,0:T(8,128)S(1)} copy-done((f32[3,2,48,128]{3,2,1,0:T(8,128)S(1)}, f32[3,2,48,128]{3,2,1,0:T(8,128)}, u32[]{:S(2)}) %copy-start.2) | copy-done | bytes 147480
  3.7 0.0 copy-start.3
  3.7 0.7 copy-done.3
  4.4 69.5 %shard_map.68 = (f32[6,48,2,8,128]{4,3,2,1,0:T(8,128)}, f32[6,48,2,8,128]{4,3,2,1,0:T(8,128)}) custom-call(f32[6,48,2,8,128]{4,3,2,1,0:T(8,128)} %bitcast.9, f32[4,18,2,8,128]{4,3,2,1,0:T(8,128)S(1)} %bitcast.6, f32[4,18,2,8,128]{4,3,2,1,0:T(8,128)S(1)} %bitcast.7, f32[288,128]{1,0:T(8,128)S(1)} %bitcast.8, s32[4,128]{1,0:T(4,128)S(1)} %copy-done.3), custom_call_target="tpu_custom_call" | custom-call | tf_op jit(solution)/shard_map/pallas_call | solution.py:323
  73.9 0.0 copy-start.4
  73.9 3.5 %copy.9 = f32[3,2,48,2,8,128]{5,4,3,2,1,0:T(8,128)} copy(f32[3,2,48,2,8,128]{5,4,3,2,1,0:T(8,128)} %bitcast.11) | data formatting | bytes 4718592
  77.4 0.0 copy-done.4
  77.4 1.4 %copy.10 = f32[3,2,48,2,8,128]{5,4,3,2,1,0:T(8,128)} copy(f32[3,2,48,2,8,128]{5,4,3,2,1,0:T(8,128)S(1)} %bitcast.10) | data formatting | bytes 4718592
Async XLA Ops:
  0.6 1.1 %copy-start = (f32[4,3,3,2,2,8,128]{6,5,4,3,2,1,0:T(8,128)S(1)}, f32[4,3,3,2,2,8,128]{6,5,4,3,2,1,0:T(8,128)}, u32[]{:S(2)}) copy-start(f32[4,3,3,2,2,8,128]{6,5,4,3,2,1,0:T(8,128)} %param.6) | copy-start | bytes 1769476
  1.7 1.1 %copy-start.1 = (f32[4,3,3,2,2,8,128]{6,5,4,3,2,1,0:T(8,128)S(1)}, f32[4,3,3,2,2,8,128]{6,5,4,3,2,1,0:T(8,128)}, u32[]{:S(2)}) copy-start(f32[4,3,3,2,2,8,128]{6,5,4,3,2,1,0:T(8,128)} %param.7) | copy-start | bytes 1769476
  2.8 0.9 %copy-start.2 = (f32[3,2,48,128]{3,2,1,0:T(8,128)S(1)}, f32[3,2,48,128]{3,2,1,0:T(8,128)}, u32[]{:S(2)}) copy-start(f32[3,2,48,128]{3,2,1,0:T(8,128)} %param.8) | copy-start | bytes 442372
  3.7 0.7 copy-start.3
  73.9 3.5 %copy-start.4 = (f32[6,48,2,8,128]{4,3,2,1,0:T(8,128)S(1)}, f32[6,48,2,8,128]{4,3,2,1,0:T(8,128)}, u32[]{:S(2)}) copy-start(f32[6,48,2,8,128]{4,3,2,1,0:T(8,128)} %get-tuple-element.5) | copy-start | bytes 7077892
where the time goes:
time: 79.1 us; the launch traced here: 78.8 us
  Pallas kernels  69.5 us (88%)
  local copies, waits for them, and re-layouts  8.63 us (11%)
    pallas_call x1, Pallas kernels, shards(): pl.pallas_call(functools.partial(kernel, n_ta, n_sa), out_shape=(jax.Shap...  69.5 us
    unnamed x12, local copies, waits for them, and re-layouts  8.63 us

commit v1 on v0

--- a/solution.py
+++ b/solution.py
@@ -35,11 +35,11 @@
 
 def kernel(
     n_ta, n_sa,
-    adj, late, mid, val, coord,
+    adj, late_in, mid_in, val, coord_in,
     two, one,
-    top, inj, vals, keys, key_row, val_hi, val_lo,
-    xh, ts, th, lts, lth, lxh, back,
-    send, recv, lsend, lrecv, vsend, vrecv,
+    top, late, mid, coord, inj, vals, keys, key_row, val_hi, val_lo,
+    xh, xs, ts, th, lts, lth, back,
+    send, recv, lsend, lrecv, vsend, vrecv, local,
 ):
     ta, sa = lax.axis_index("ta"), lax.axis_index("sa")
     t_up, t_dn = lax.rem(ta + 1, n_ta), lax.rem(ta + n_ta - 1, n_ta)
@@ -49,6 +49,14 @@
     planes = 2 * n_sa
     links = (late, mid)
 
+    loads = [
+        pltpu.make_async_copy(src, dst, local.at[i])
+        for i, (src, dst) in enumerate(
+            ((coord_in, coord), (val, vals.at[0, 0]), (adj, top), (late_in, late), (mid_in, mid))
+        )
+    ]
+    for load in loads:
+        load.start()
     barrier = pltpu.get_barrier_semaphore()
     for step in range(1, n_sa):
         pl.semaphore_signal(
@@ -64,10 +72,15 @@
         )
 
     def x_copy(lap, way, k):
-        field = adj if lap == 0 else two
         cut = pl.ds(k * COLS, COLS)
+        if way == 1:
+            src = xs.at[lap, :, cut]
+        elif lap == 0:
+            src = adj.at[:, cut, 0]
+        else:
+            src = two.at[:, cut, 0]
         return remote(
-            field.at[:, cut, way], xh.at[lap, way, :, cut],
+            src, xh.at[lap, way, :, cut],
             send.at[lap, way, k], recv.at[lap, way, k], {"sa": x_up if way else x_dn},
         )
 
@@ -77,13 +90,8 @@
             send.at[lap, 2 + way, k], recv.at[lap, 2 + way, k], {"ta": t_up if way else t_dn},
         )
 
-    def lx_copy(lap):
-        return remote(
-            links[lap].at[1, :, 1], lxh.at[lap], lsend.at[lap, 0], lrecv.at[lap, 0], {"sa": x_up}
-        )
-
     def lt_copy(lap):
-        return remote(lts.at[lap], lth.at[lap], lsend.at[lap, 1], lrecv.at[lap, 1], {"ta": t_up})
+        return remote(lts.at[lap], lth.at[lap], lsend.at[lap], lrecv.at[lap], {"ta": t_up})
 
     core = lax.rem(sa, 2)
     chip = sa // 2
@@ -102,32 +110,37 @@
             remote(src_k, keys.at[kind, step], vsend.at[kind, step, 1], vrecv.at[kind, step, 1], {"sa": peer}),
         )
 
-    vals[0, 0] = val[...]
+    loads[0].wait()
     key = (coord[1:2, :] * 8 + coord[0:1, :] - ta * 8) * 128 + coord[2:3, :] * EXTENT_Z + coord[3:4, :]
     keys[0, 0] = jnp.broadcast_to(key, (8, records))
+    loads[1].wait()
     for step in range(1, n_chip):
         for c in rec_copies(0, step):
             c.start()
     for c in rec_copies(1, 0):
         c.start()
-    lx_copy(0).start()
-
-    @pl.loop(0, chunks)
+
+    @pl.loop(0, chunks // 3)
     def _(k):
         x_copy(0, 0, k).start()
-        x_copy(0, 1, k).start()
-
+
+    for load in loads[2:]:
+        load.wait()
     for lap in range(2):
         flat = links[lap].reshape(4 * 18 * 2 * 8, 128)
         lts[lap] = flat[pl.ds(7, 40, stride=8), :]
         lt_copy(lap).start()
-    lx_copy(1).start()
 
     for step in range(1, n_chip):
         for c in rec_copies(0, step):
             c.wait_recv()
         for c in rec_copies(1, step):
             c.start()
+
+    @pl.loop(chunks // 3, chunks)
+    def _(k):
+        x_copy(0, 0, k).start()
+
     for step in range(n_chip):
         for c in rec_copies(1, step):
             c.wait_recv()
@@ -141,19 +154,13 @@
             key_row[:, at : at + records] = keys[kind, step]
 
     top_flat = top.reshape(288 * 16, 128)
-    adj_flat = adj.reshape(288 * 16, 128)
     width = key_row.shape[1]
     dims = (((1,), (1,)), ((), ()))
 
     @pl.loop(0, 4)
     def _(pair):
-        for plane in range(4):
-            if plane < 2:
-                x_at = sa * 2 + plane
-            elif plane == 2:
-                x_at = x_up * 2
-            else:
-                x_at = x_dn * 2 + 1
+        for plane in range(3):
+            x_at = sa * 2 + plane if plane < 2 else x_up * 2
             first = (x_at * 8 + pair * 2) * 128
             site = lax.broadcasted_iota(jnp.int32, (256, width), 0) + first
             hot = jnp.where(site == key_row[0:1, :], 1.0, 0.0).astype(jnp.bfloat16)
@@ -164,9 +171,9 @@
                 t_at = pair * 2 + half
                 if plane < 2:
                     rows = pl.ds(plane * 8 + t_at, 288, stride=16)
-                    top_flat[rows, :] = adj_flat[rows, :] + part
+                    top_flat[rows, :] = top_flat[rows, :] + part
                 else:
-                    inj.at[plane - 2].reshape(288 * 8, 128)[pl.ds(t_at, 288, stride=8), :] = part
+                    inj.reshape(288 * 8, 128)[pl.ds(t_at, 288, stride=8), :] = part
 
     sign_dn = jnp.where(ta == 0, -1.0, 1.0).astype(jnp.float32)
     sign_up = jnp.where(ta == n_ta - 1, -1.0, 1.0).astype(jnp.float32)
@@ -180,8 +187,19 @@
         t_copy(lap, 0, k).start()
         t_copy(lap, 1, k).start()
 
+    def send_back(lap, k):
+        field, link = (top if lap == 0 else two), links[lap]
+        vec = [[field[q, k * COLS + j, 1] for j in range(COLS)] for q in range(6)]
+        acc = [[jnp.zeros((8, 128), jnp.float32)] * COLS for _ in range(6)]
+        mac(acc, lambda r, c, p: link[1, (r * 3 + c) * 2 + p, 1], vec, True)
+        for q in range(6):
+            for j in range(COLS):
+                xs[lap, q, k * COLS + j] = acc[q][j]
+        x_copy(lap, 1, k).start()
+
     @pl.loop(0, chunks)
     def _(k):
+        send_back(0, k)
         send_time(0, k)
 
     row = lax.broadcasted_iota(jnp.int32, (8, 128), 0)
@@ -200,7 +218,6 @@
         return jnp.where(z_at == 0, pltpu.roll(a, 129 - EXTENT_Z, 1), pltpu.roll(a, 1, 1))
 
     for lap in range(2):
-        lx_copy(lap).wait_recv()
         lt_copy(lap).wait_recv()
 
         @pl.loop(0, 18)
@@ -209,9 +226,8 @@
             for x in range(2):
                 edge = lth[lap, pl.ds(e * 2 + x, 1), :]
                 back[lap, 0, e, x] = jnp.where(row == 0, edge, pltpu.roll(link[0, e, x], 1, 0))
-                back[lap, 1, e, x] = lxh[lap, e] if x == 0 else link[1, e, 0]
-                back[lap, 2, e, x] = y_behind(link[2, e, x])
-                back[lap, 3, e, x] = z_behind(link[3, e, x])
+                back[lap, 1, e, x] = y_behind(link[2, e, x])
+                back[lap, 2, e, x] = z_behind(link[3, e, x])
 
     def laplacian(lap, k, x):
         field = top if lap == 0 else two
@@ -220,19 +236,16 @@
         def ahead(mu):
             return lambda r, c, p: link[mu, (r * 3 + c) * 2 + p, x]
 
-        def behind(mu):
-            return lambda r, c, p: back[lap, mu, (r * 3 + c) * 2 + p, x]
+        def behind(which):
+            return lambda r, c, p: back[lap, which, (r * 3 + c) * 2 + p, x]
 
         def here(plane):
             return [[field[q, k * COLS + j, plane] for j in range(COLS)] for q in range(6)]
 
         def halo(way):
             vec = [[xh[lap, way, q, k * COLS + j] for j in range(COLS)] for q in range(6)]
-            if lap == 0:
-                side = 0 if way == 0 else 1
-                vec = [
-                    [vec[q][j] + inj[side, q * 48 + k * COLS + j] for j in range(COLS)] for q in range(6)
-                ]
+            if lap == 0 and way == 0:
+                vec = [[vec[q][j] + inj[q * 48 + k * COLS + j] for j in range(COLS)] for q in range(6)]
             return vec
 
         def moved(f, vec):
@@ -256,13 +269,16 @@
         centre = here(x)
         acc = [[-8.0 * a for a in line] for line in centre]
         mac(acc, ahead(2), moved(y_ahead, centre), False)
-        mac(acc, behind(2), moved(y_behind, centre), True)
+        mac(acc, behind(1), moved(y_behind, centre), True)
         mac(acc, ahead(3), moved(z_ahead, centre), False)
-        mac(acc, behind(3), moved(z_behind, centre), True)
+        mac(acc, behind(2), moved(z_behind, centre), True)
         mac(acc, ahead(0), time(0, centre), False)
         mac(acc, behind(0), time(1, centre), True)
         mac(acc, ahead(1), here(1) if x == 0 else halo(0), False)
-        mac(acc, behind(1), halo(1) if x == 0 else here(0), True)
+        if x == 0:
+            hop = halo(1)
+            return [[acc[q][j] + hop[q][j] for j in range(COLS)] for q in range(6)]
+        mac(acc, lambda r, c, p: link[1, (r * 3 + c) * 2 + p, 0], here(0), True)
         return acc
 
     def arrive(lap, k):
@@ -279,7 +295,7 @@
                 for j in range(COLS):
                     two[q, k * COLS + j, x] = coef_late * acc[q][j]
         x_copy(1, 0, k).start()
-        x_copy(1, 1, k).start()
+        send_back(1, k)
         send_time(1, k)
 
     @pl.loop(0, chunks)
@@ -298,7 +314,6 @@
             for c in rec_copies(0, step):
                 c.wait_send()
     for lap in range(2):
-        lx_copy(lap).wait_send()
         lt_copy(lap).wait_send()
 
         @pl.loop(0, chunks)
@@ -322,33 +337,37 @@
     vmem = pl.BlockSpec(memory_space=pltpu.VMEM)
     two, one = pl.pallas_call(
         functools.partial(kernel, n_ta, n_sa),
-        out_shape=(jax.ShapeDtypeStruct(adj.shape, f32), jax.ShapeDtypeStruct(adj.shape, f32)),
-        in_specs=[vmem] * 5,
+        out_shape=(pltpu.VMEM(adj.shape, f32), pltpu.VMEM(adj.shape, f32)),
+        in_specs=[pl.BlockSpec(memory_space=pl.ANY)] * 5,
         out_specs=(vmem, vmem),
         scratch_shapes=[
             pltpu.VMEM(adj.shape, f32),
-            pltpu.VMEM((2, 6 * cols, 8, 128), f32),
+            pltpu.VMEM(late.shape, f32),
+            pltpu.VMEM(mid.shape, f32),
+            pltpu.VMEM(src_coord.shape, jnp.int32),
+            pltpu.VMEM((6 * cols, 8, 128), f32),
             pltpu.VMEM((2, n_sa // 2, 6 * cols, records), f32),
             pltpu.VMEM((2, n_sa // 2, 8, records), jnp.int32),
             pltpu.VMEM((8, width), jnp.int32),
             pltpu.VMEM((6 * cols, width), jnp.bfloat16),
             pltpu.VMEM((6 * cols, width), jnp.bfloat16),
             pltpu.VMEM((2, 2, 6, cols, 8, 128), f32),
+            pltpu.VMEM((2, 6, cols, 8, 128), f32),
             pltpu.VMEM((2, 2, chunks, 6, 2 * COLS, 128), f32),
             pltpu.VMEM((2, 2, chunks, 6, 2 * COLS, 128), f32),
             pltpu.VMEM((2, 40, 128), f32),
             pltpu.VMEM((2, 40, 128), f32),
-            pltpu.VMEM((2, 18, 8, 128), f32),
-            pltpu.VMEM((2, 4, 18, 2, 8, 128), f32),
+            pltpu.VMEM((2, 3, 18, 2, 8, 128), f32),
             dma((2, 4, chunks)),
             dma((2, 4, chunks)),
-            dma((2, 2)),
-            dma((2, 2)),
+            dma((2,)),
+            dma((2,)),
             dma((2, n_sa // 2, 2)),
             dma((2, n_sa // 2, 2)),
+            dma((5,)),
         ],
         compiler_params=pltpu.CompilerParams(
-            collective_id=0, has_side_effects=True, vmem_limit_bytes=52 * 1024 * 1024
+            collective_id=0, has_side_effects=True, vmem_limit_bytes=56 * 1024 * 1024
         ),
     )(adj, late, mid, val, src_coord)
     return two.reshape(adjoint_in.shape), one.reshape(adjoint_in.shape)

time: 79.1 us -> 68.4 us (0.86)
  the two profiles are of different devices: /device:TPU:1 before, /device:TPU:0 now
where the time goes in v1:
time: 68.4 us; the launch traced here: 68.3 us
  Pallas kernels  64.8 us (95%)
  local copies, waits for them, and re-layouts  2.81 us (4%)
    pallas_call x1, Pallas kernels, shards(): pl.pallas_call(functools.partial(kernel, n_ta, n_sa), out_shape=(pltpu.VM...  64.8 us
    unnamed x2, local copies, waits for them, and re-layouts  2.81 us

profile of v1, /device:TPU:0, one launch (start us, length us, event | category | flops | bytes accessed | tf_op | source)
XLA Modules:
  0.0 68.3 jit_solution(3564635072378597045)
XLA Ops:
  0.6 64.8 %shard_map.68 = (f32[6,48,2,8,128]{4,3,2,1,0:T(8,128)S(1)}, f32[6,48,2,8,128]{4,3,2,1,0:T(8,128)S(1)}) custom-call(f32[6,48,2,8,128]{4,3,2,1,0:T(8,128)} %bitcast.8, f32[4,18,2,8,128]{4,3,2,1,0:T(8,128)} %bitcast.9, f32[4,18,2,8,128]{4,3,2,1,0:T(8,128)} %bitcast.10, f32[288,128]{1,0:T(8,128)} %bitcast.11, s32[4,128]{1,0:T(4,128)} %coord_in.1), custom_call_target="tpu_custom_call" | custom-call | tf_op jit(solution)/shard_map/pallas_call | solution.py:338
  65.5 1.4 %copy.9 = f32[3,2,48,2,8,128]{5,4,3,2,1,0:T(8,128)} copy(f32[3,2,48,2,8,128]{5,4,3,2,1,0:T(8,128)S(1)} %bitcast.7) | data formatting | bytes 4718592
  66.9 1.4 %copy.10 = f32[3,2,48,2,8,128]{5,4,3,2,1,0:T(8,128)} copy(f32[3,2,48,2,8,128]{5,4,3,2,1,0:T(8,128)S(1)} %bitcast.6) | data formatting | bytes 4718592

commit v2 on v1

--- a/solution.py
+++ b/solution.py
@@ -49,6 +49,13 @@
     planes = 2 * n_sa
     links = (late, mid)
 
+    barrier = pltpu.get_barrier_semaphore()
+    for step in range(1, n_sa):
+        pl.semaphore_signal(
+            barrier, inc=1, device_id={"sa": lax.rem(sa + step, n_sa)}, device_id_type=MESH
+        )
+    for other in (t_up, t_dn):
+        pl.semaphore_signal(barrier, inc=1, device_id={"ta": other}, device_id_type=MESH)
     loads = [
         pltpu.make_async_copy(src, dst, local.at[i])
         for i, (src, dst) in enumerate(
@@ -57,13 +64,6 @@
     ]
     for load in loads:
         load.start()
-    barrier = pltpu.get_barrier_semaphore()
-    for step in range(1, n_sa):
-        pl.semaphore_signal(
-            barrier, inc=1, device_id={"sa": lax.rem(sa + step, n_sa)}, device_id_type=MESH
-        )
-    for other in (t_up, t_dn):
-        pl.semaphore_signal(barrier, inc=1, device_id={"ta": other}, device_id_type=MESH)
     pl.semaphore_wait(barrier, n_sa + 1)
 
     def remote(src, dst, s, r, where):
@@ -370,6 +370,27 @@
             collective_id=0, has_side_effects=True, vmem_limit_bytes=56 * 1024 * 1024
         ),
     )(adj, late, mid, val, src_coord)
+    def write_out(two_ref, one_ref, two_out, one_out, sem):
+        copies = [
+            pltpu.make_async_copy(src.at[q], dst.at[q], sem.at[i, q])
+            for q in range(6)
+            for i, (src, dst) in enumerate(((two_ref, two_out), (one_ref, one_out)))
+        ]
+        for c in copies:
+            c.start()
+        for c in copies:
+            c.wait()
+
+    out = jax.ShapeDtypeStruct(adj.shape, f32)
+    hbm = pl.BlockSpec(memory_space=pl.ANY)
+    two, one = pl.pallas_call(
+        write_out,
+        out_shape=(out, out),
+        in_specs=[vmem, vmem],
+        out_specs=(hbm, hbm),
+        scratch_shapes=[dma((2, 6))],
+        compiler_params=pltpu.CompilerParams(vmem_limit_bytes=1024 * 1024),
+    )(two, one)
     return two.reshape(adjoint_in.shape), one.reshape(adjoint_in.shape)
 
 

time: 68.4 us -> 67.9 us (level)
  local copies, waits for them, and re-layouts: 2.81 us -> 0 us
  Pallas kernels: 64.8 us -> 67.1 us
    unnamed x2 -> x0, local copies, waits for them, and re-layouts: 2.81 us -> none
    pallas_call x0 -> x1, Pallas kernels: none -> 2.27 us  [shards(): pl.pallas_call(write_out, out_shape=(out, out), in_specs=[vmem, vmem], ou...]
where the time goes in v2:
time: 67.9 us; the launch traced here: 67.7 us
  Pallas kernels  67.1 us (99%)
    pallas_call x1, Pallas kernels, shards(): pl.pallas_call(functools.partial(kernel, n_ta, n_sa), out_shape=(pltpu.VM...  64.8 us
    pallas_call x1, Pallas kernels, shards(): pl.pallas_call(write_out, out_shape=(out, out), in_specs=[vmem, vmem], ou...  2.27 us

profile of v2, /device:TPU:0, one launch (start us, length us, event | category | flops | bytes accessed | tf_op | source)
XLA Modules:
  0.0 67.7 jit_solution(9456033875404500688)
XLA Ops:
  0.6 64.8 %shard_map.68 = (f32[6,48,2,8,128]{4,3,2,1,0:T(8,128)S(1)}, f32[6,48,2,8,128]{4,3,2,1,0:T(8,128)S(1)}) custom-call(f32[6,48,2,8,128]{4,3,2,1,0:T(8,128)} %bitcast.6, f32[4,18,2,8,128]{4,3,2,1,0:T(8,128)} %bitcast.7, f32[4,18,2,8,128]{4,3,2,1,0:T(8,128)} %bitcast.8, f32[288,128]{1,0:T(8,128)} %bitcast.9, s32[4,128]{1,0:T(4,128)} %coord_in.1), custom_call_target="tpu_custom_call" | custom-call | tf_op jit(solution)/shard_map/pallas_call | solution.py:338
  65.5 2.3 %shard_map.69 = (f32[6,48,2,8,128]{4,3,2,1,0:T(8,128)}, f32[6,48,2,8,128]{4,3,2,1,0:T(8,128)}) custom-call(f32[6,48,2,8,128]{4,3,2,1,0:T(8,128)S(1)} %get-tuple-element.6.two_ref, f32[6,48,2,8,128]{4,3,2,1,0:T(8,128)S(1)} %get-tuple-element.7.one_ref), custom_call_target="tpu_custom_call" | custom-call | tf_op jit(solution)/shard_map/pallas_call | solution.py:386
